TPU v7x, 32 devices: a whole 2x2x4 slice. The times are simulated.
32 devices in a mesh: slab: 2 (over x), blk: 16 (over z, y, core).
Axes of the slice: x: 2, y: 2, z: 4, core: 2. Of those that a mesh axis runs over, the one named last changes fastest.
Arguments:
- expression: bfloat16 [768, 4096], P('blk', 'slab'), parts along dimension 1, may hold values from -400 to 400
- dosages: bfloat16 [768, 32768], P(None, ('slab', 'blk')), parts along dimension 1, may hold values from -400 to 400
- covariates: float32 [64, 768], replicated, may hold values from -6 to 6
- window_blocks: int32 [32, 16], P(('slab', 'blk')), parts along dimension 0, may hold values from 0 to 127, as said below
- window_counts: int32 [32], P(('slab', 'blk')), parts along dimension 0, may hold values from 10 to 16
Outputs:
- scores: float32 [32, 16, 128, 128], P(('slab', 'blk')), parts along dimension 0
There are 2 independent parts, one for each index of `slab`. A program takes and returns all parts, laid end to end along the dimension named above; an argument that names none is the same for every part. Nothing has to cross between parts.
Inputs may be any that keep to these rules, and one draw needn't show every extreme that they name: `window_blocks`: row b lists window_counts[b] consecutive variant blocks followed by repeats of its first, all among the variant blocks of the device that owns gene block b (block b) and of its two neighbours.
All inputs are finite; a program needn't handle non-finite values.
Results may differ from a plain program's by a relative error of at most 0.0039.
Values may be sent and summed in bfloat16 or wider, within the bound.
A program may use at most 128 MiB of HBM per device.

v0:
```python
import math

import jax
import jax.numpy as jnp
from jax import lax
from jax.sharding import PartitionSpec as P

BS = 128


def extended_2(block, sides, width):
    for axis, dim in sides:
        count = lax.axis_size(axis)
        forward = [(i, i + 1) for i in range(count - 1)]
        backward = [(target, source) for source, target in forward]
        low = lax.ppermute(
            lax.slice_in_dim(block, block.shape[dim] - width, None, axis=dim), axis, forward
        )
        high = lax.ppermute(lax.slice_in_dim(block, 0, width, axis=dim), axis, backward)
        block = jnp.concatenate([low, block, high], axis=dim)
    return block


def residualize(values, covariates, factor):
    projected = jnp.dot(covariates, values, precision=lax.Precision.HIGHEST)
    middle = lax.linalg.triangular_solve(
        factor, projected, left_side=True, lower=True, transpose_a=False
    )
    coefficients = lax.linalg.triangular_solve(
        factor, middle, left_side=True, lower=True, transpose_a=True
    )
    residuals = values - jnp.dot(covariates.T, coefficients, precision=lax.Precision.HIGHEST)
    column_scale = lax.rsqrt(jnp.mean(residuals * residuals, axis=0) + 1e-06)
    return (residuals * column_scale).astype(jnp.bfloat16)


def listed_products(extended, gene_ready, local_index):
    samples_all = extended.shape[0]
    gene_count, slot_count = local_index.shape
    panels = extended.reshape(samples_all, extended.shape[1] // BS, BS)
    chosen = jnp.take(panels, local_index.reshape(-1), axis=1)
    chosen = chosen.reshape(samples_all, gene_count, slot_count * BS)
    gene_block_data = gene_ready.reshape(samples_all, gene_count, BS)
    product = jnp.einsum(
        "nim,nig->img", chosen, gene_block_data, preferred_element_type=jnp.float32
    )
    return product.reshape(gene_count, slot_count, BS, BS)


def on_device(expression, dosages, covariates, window_blocks, window_counts):
    position = lax.axis_index("blk")
    factor = jnp.linalg.cholesky(jnp.dot(covariates, covariates.T, precision=lax.Precision.HIGHEST))
    gene_columns = lax.all_to_all(expression, "blk", split_axis=1, concat_axis=0, tiled=True)
    samples_all = gene_columns.shape[0]
    panel_width = dosages.shape[1]
    panel_count = panel_width // BS
    local_index = window_blocks - (position - 1) * panel_count
    gene_ready = residualize(gene_columns.astype(jnp.float32), covariates, factor)
    panel_ready = residualize(dosages.astype(jnp.float32), covariates, factor)
    extended = extended_2(panel_ready, (("blk", 1),), panel_width)
    product_blocks = listed_products(extended, gene_ready, local_index)
    factor_z = math.sqrt(samples_all - covariates.shape[0]) / samples_all
    live_slots = jnp.arange(local_index.shape[1])[None, :] < window_counts[:, None]
    return jnp.where(live_slots[:, :, None, None], product_blocks * factor_z, 0.0)


def solution(mesh):
    in_specs = (
        P("blk", "slab"),
        P(None, ("slab", "blk")),
        P(),
        P(("slab", "blk"), None),
        P(("slab", "blk")),
    )
    out_specs = P(("slab", "blk"), None, None, None)
    return jax.shard_map(
        on_device, mesh=mesh, in_specs=in_specs, out_specs=out_specs, check_vma=False
    )
```

profile of v0, /device:TPU:1, one launch (start us, length us, event | category | flops | bytes accessed | tf_op | source)
XLA Modules:
  0.0 75.4 jit_solution(30717350333852436)
XLA Ops:
  0.0 0.9 %copy-done = f32[64,768]{1,0:T(8,128)S(1)} copy-done((f32[64,768]{1,0:T(8,128)S(1)}, f32[64,768]{1,0:T(8,128)}, u32[]{:S(2)}) %copy-start) | copy-done | bytes 196632
  0.9 0.3 fusion.17
  1.2 3.0 %fusion.18 = f32[64,1024]{1,0:T(8,128)} fusion(f32[64,768]{1,0:T(8,128)S(1)} %copy-done, bf16[768,1024]{1,0:T(8,128)(2,1)} %param.6), kind=kOutput, calls=%fused_computation.42 | convolution fusion | flops 603979776 | bytes 2031616 | tf_op jit(solution)/shard_map/dot_general | solution.py:25
  4.3 0.7 copy.19
  5.0 0.1 copy.20
  5.1 5.8 %cholesky.16 = f32[64,64]{1,0:T(8,128)S(1)} custom-call(f32[64,64]{1,0:T(8,128)S(1)} %fusion.15), custom_call_target="Cholesky" | custom-call | tf_op jit(solution)/shard_map/jit(cholesky)/cholesky | solution.py:52
  11.0 0.7 compare_reduce_fusion
  11.7 0.7 fusion.6
  12.4 4.9 %custom-call.12 = f32[1,64,64]{1,2,0:T(8,128)S(1)} custom-call(f32[1,64,64]{2,1,0:T(8,128)S(1)} %fusion.6), custom_call_target="InvertDiagBlocksLowerTriangular" | custom-call | tf_op jit(solution)/shard_map/triangular_solve | solution.py:29
  17.3 1.4 %fusion.13 = f32[64,1024]{1,0:T(8,128)S(1)} fusion(f32[64,1024]{1,0:T(8,128)} %fusion.18, f32[1,64,64]{1,2,0:T(8,128)S(1)} %custom-call.12), kind=kOutput, calls=%fused_computation.24 | convolution fusion | flops 50331648 | bytes 540672 | tf_op jit(solution)/shard_map/triangular_solve | solution.py:26
  18.7 0.4 fusion.11
  19.1 3.0 %multiply_reduce_fusion = (f32[1024]{0:T(1024)S(1)}, f32[1024,768]{1,0:T(8,128)S(1)}) fusion(bf16[768,1024]{0,1:T(8,128)(2,1)S(1)} %copy.19, f32[64,1024]{1,0:T(8,128)S(1)} %fusion.11, f32[64,768]{1,0:T(8,128)S(1)} %copy-done), kind=kOutput, calls=%fused_computation.5 | convolution fusion | flops 607124480 | bytes 5181440 | tf_op jit(solution)/shard_map/dot_general | solution.py:32
  22.0 0.0 copy-start.3
  22.0 0.0 copy-start.4
  22.0 0.4 multiply_convert_fusion
  22.5 4.5 %collective-permute-start = (bf16[768,1024]{0,1:T(8,128)(2,1)S(1)}, bf16[768,1024]{0,1:T(8,128)(2,1)}, u32[]{:S(2)}, u32[]{:S(2)}) collective-permute-start(bf16[768,1024]{0,1:T(8,128)(2,1)S(1)} %multiply_convert_fusion), channel_id=1, source_target_pairs={{0,1},{1,2},{2,3},{3,4},{4,5},{5,6},{6,7},{7,8},{8,9},{9,10},{10,1... | collective-permute-start | bytes 4718600 | tf_op jit(solution)/shard_map/ppermute | solution.py:16
  27.0 1.9 %collective-permute-start.1 = (bf16[768,1024]{0,1:T(8,128)(2,1)S(1)}, bf16[768,1024]{0,1:T(8,128)(2,1)}, u32[]{:S(2)}, u32[]{:S(2)}) collective-permute-start(bf16[768,1024]{0,1:T(8,128)(2,1)S(1)} %multiply_convert_fusion), channel_id=1, source_target_pairs={{1,0},{2,1},{3,2},{4,3},{5,4},{6,5},{7,6},{8,7},{9,8},{10,9},{11,1... | collective-permute-start | bytes 4718600 | tf_op jit(solution)/shard_map/ppermute | solution.py:19
  28.9 0.7 copy_bitcast_fusion
  29.7 6.4 %all-to-all-start = ((bf16[48,16,128]{2,0,1:T(8,128)(2,1)}), bf16[48,16,128]{2,0,1:T(8,128)(2,1)S(1)}, u32[]{:S(2)}, u32[]{:S(2)}) async-start(bf16[48,16,128]{2,0,1:T(8,128)(2,1)} %copy_bitcast_fusion), calls=%async_computation | async-start | bytes 393216 | tf_op jit(solution)/shard_map/all_to_all | solution.py:53
  36.8 0.1 broadcast_bitcast_fusion
  36.9 26.4 %all-to-all-done = bf16[48,16,128]{2,0,1:T(8,128)(2,1)S(1)} async-done(((bf16[48,16,128]{2,0,1:T(8,128)(2,1)}), bf16[48,16,128]{2,0,1:T(8,128)(2,1)S(1)}, u32[]{:S(2)}, u32[]{:S(2)}) %all-to-all-start) | async-done | bytes 196640 | tf_op jit(solution)/shard_map/all_to_all | solution.py:53
  63.3 0.1 copy.22
  63.5 0.2 fusion.19
  63.7 0.2 fusion.9
  63.9 0.2 fusion.7
  64.1 1.3 %multiply_reduce_fusion.1 = (f32[128]{0:T(128)S(1)}, f32[768,128]{0,1:T(8,128)}) fusion(f32[64,128]{1,0:T(8,128)S(1)} %fusion.7, f32[64,768]{1,0:T(8,128)S(1)} %copy-done, bf16[768,128]{0,1:T(8,128)(2,1)S(1)} %copy.22), kind=kOutput, calls=%fused_computation.12 | convolution fusion | flops 75890560 | bytes 819712 | tf_op jit(solution)/shard_map/dot_general | solution.py:32
  65.4 3.9 %pad_maximum_fusion = bf16[768,3072]{0,1:T(8,128)(2,1)} fusion(bf16[768,1024]{0,1:T(8,128)(2,1)} %collective-permute-done.1, bf16[768,1024]{0,1:T(8,128)(2,1)S(1)} %multiply_convert_fusion, bf16[768,1024]{0,1:T(8,128)(2,1)} %collective-permute-done), kind=kLoop, calls=%fused_computation.1 | loop fusion | flops 14155776 | bytes 9437184 | tf_op jit(solution)/shard_map/concatenate | solution.py:20
  69.3 3.1 %gather_fusion = bf16[16,768,128]{1,2,0:T(8,128)(2,1)S(1)} fusion(bf16[768,24,128]{0,2,1:T(8,128)(2,1)} %bitcast.71, s32[1024]{0:T(1024)S(1)} %pad_clamp_fusion), kind=kCustom, calls=%fused_computation | custom fusion | bytes 6291520 | tf_op jit(solution)/shard_map/jit(_take)/gather | solution.py:41
  72.4 0.0 copy-start.2
  72.4 0.7 bitcast_select_fusion
  73.1 0.3 copy-done.2
  73.4 2.0 %fusion.1 = f32[1,16,128,128]{3,2,1,0:T(8,128)} fusion(bf16[16,128,768]{2,1,0:T(8,128)(2,1)S(1)} %bitcast.72, pred[16]{0:T(512)(128)(4,1)S(1)} %iota_compare_fusion.2, f32[768,128]{0,1:T(8,128)S(1)} %copy-done.2, f32[128]{0:T(128)S(1)} %add_rsqrt_fusion.1), kind=kOutput, calls=%fused_computation.8 | convolution fusion | flops 403374080 | bytes 4588048 | tf_op jit(solution)/shard_map/nim,nig->img/dot_general | solution.py:44
  (15 shorter events, 0.1 us)
Async XLA Ops:
  0.0 0.9 %copy-start = (f32[64,768]{1,0:T(8,128)S(1)}, f32[64,768]{1,0:T(8,128)}, u32[]{:S(2)}) copy-start(f32[64,768]{1,0:T(8,128)} %param.7) | copy-start | bytes 589828
  0.0 4.3 %copy-start.1 = (bf16[768,1024]{1,0:T(8,128)(2,1)S(1)}, bf16[768,1024]{1,0:T(8,128)(2,1)}, u32[]{:S(2)}) copy-start(bf16[768,1024]{1,0:T(8,128)(2,1)} %param.6) | copy-start | bytes 4718596
  22.0 6.9 %copy-start.3 = (bf16[48,2048]{1,0:T(8,128)(2,1)S(1)}, bf16[48,2048]{1,0:T(8,128)(2,1)}, u32[]{:S(2)}) copy-start(bf16[48,2048]{1,0:T(8,128)(2,1)} %param.5) | copy-start | bytes 589828
  22.0 14.1 %copy-start.4 = (s32[1,16]{1,0:T(1,128)S(1)}, s32[1,16]{1,0:T(1,128)}, u32[]{:S(2)}) copy-start(s32[1,16]{1,0:T(1,128)} %param.8) | copy-start | bytes 196
  22.5 43.0 %collective-permute-start = (bf16[768,1024]{0,1:T(8,128)(2,1)S(1)}, bf16[768,1024]{0,1:T(8,128)(2,1)}, u32[]{:S(2)}, u32[]{:S(2)}) collective-permute-start(bf16[768,1024]{0,1:T(8,128)(2,1)S(1)} %multiply_convert_fusion), channel_id=1, source_target_pairs={{0,1},{1,2},{2,3},{3,4},{4,5},{5,6},{6,7},{7,8},{8,9},{9,10},{10,1... | collective-permute-start | bytes 4718600 | tf_op jit(solution)/shard_map/ppermute | solution.py:16
  27.0 38.4 %collective-permute-start.1 = (bf16[768,1024]{0,1:T(8,128)(2,1)S(1)}, bf16[768,1024]{0,1:T(8,128)(2,1)}, u32[]{:S(2)}, u32[]{:S(2)}) collective-permute-start(bf16[768,1024]{0,1:T(8,128)(2,1)S(1)} %multiply_convert_fusion), channel_id=1, source_target_pairs={{1,0},{2,1},{3,2},{4,3},{5,4},{6,5},{7,6},{8,7},{9,8},{10,9},{11,1... | collective-permute-start | bytes 4718600 | tf_op jit(solution)/shard_map/ppermute | solution.py:19
  29.7 33.6 %all-to-all-start = ((bf16[48,16,128]{2,0,1:T(8,128)(2,1)}), bf16[48,16,128]{2,0,1:T(8,128)(2,1)S(1)}, u32[]{:S(2)}, u32[]{:S(2)}) async-start(bf16[48,16,128]{2,0,1:T(8,128)(2,1)} %copy_bitcast_fusion), calls=%async_computation | async-start | bytes 393216 | tf_op jit(solution)/shard_map/all_to_all | solution.py:53
  72.4 1.0 %copy-start.2 = (f32[768,128]{0,1:T(8,128)S(1)}, f32[768,128]{0,1:T(8,128)}, u32[]{:S(2)}) copy-start(f32[768,128]{0,1:T(8,128)} %get-tuple-element.8) | copy-start | bytes 1179652
where the time goes:
time: 76.7 us; the launch traced here: 75.4 us
  waiting for transfers between devices  26.4 us (34%)
  other arithmetic  17.2 us (22%)
  starting transfers between devices  12.9 us (17%)
  matrix products  12 us (16%)
  local copies, waits for them, and re-layouts  5.99 us (8%)
  between operations  0.85 us (1%)
    all_to_all x1, waiting for transfers between devices, on_device(): lax.all_to_all(expression, 'blk', split_axis=1, concat_axis=0, tiled=True)  26.4 us
    another operation x3, other arithmetic, on_device(): jnp.linalg.cholesky(jnp.dot(covariates, covariates.T, precision=lax.Preci...  6.6 us
    all_to_all x1, starting transfers between devices, on_device(): lax.all_to_all(expression, 'blk', split_axis=1, concat_axis=0, tiled=True)  6.45 us
    another operation x2, other arithmetic, residualize(): lax.linalg.triangular_solve(factor, middle, left_side=True, lower=True, t...  5.59 us
    ppermute x1, starting transfers between devices, extended_2(): lax.ppermute(lax.slice_in_dim(block, block.shape[dim] - width, None, axis...  4.54 us
    dot_general x2, matrix products, residualize(): jnp.dot(covariates.T, coefficients, precision=lax.Precision.HIGHEST)  4.24 us
    concatenate x1, other arithmetic, extended_2(): block = jnp.concatenate([low, block, high], axis=dim)  3.87 us
    dot_general x2, matrix products, residualize(): projected = jnp.dot(covariates, values, precision=lax.Precision.HIGHEST)  3.29 us
  transfers between devices with their start and end apart: 3, of which 1 were waited for; matrix products, arithmetic and copies ran while one was open for 4% of the time, Pallas kernels for 0%

commit v1 on v0

v1 whole, which is shorter than its diff:
```python
import functools
import math

import jax
import jax.numpy as jnp
from jax import lax
from jax.experimental import pallas as pl
from jax.experimental.pallas import tpu as pltpu
from jax.sharding import PartitionSpec as P

BS = 128
PANEL = 4
MESH = pl.DeviceIdType.MESH
F32 = jnp.float32
BF16 = jnp.bfloat16
NT = (((1,), (1,)), ((), ()))


def split3(x):
    high = x.astype(BF16)
    rest = x - high.astype(F32)
    middle = rest.astype(BF16)
    low = (rest - middle.astype(F32)).astype(BF16)
    return high, middle, low


def whitened(cov):
    k = cov.shape[0]
    zeros = jnp.zeros_like(cov)
    gram = lax.dot_general(
        cov,
        jnp.concatenate([cov, zeros], axis=0),
        NT,
        precision=lax.Precision.HIGHEST,
        preferred_element_type=F32,
    )
    lane = lax.broadcasted_iota(jnp.int32, (8, 2 * k), 1)
    sub = lax.broadcasted_iota(jnp.int32, (8, 2 * k), 0)
    tiles = []
    for t in range(k // 8):
        unit = (lane - k == sub + 8 * t).astype(F32)
        tiles.append(jnp.where(lane < k, gram[8 * t : 8 * t + 8, :], unit))
    for first in range(0, k, PANEL):
        home = first // 8
        live = range(home, k // 8)
        columns = [
            {t: jnp.broadcast_to(tiles[t][:, first + j : first + j + 1], (8, 2 * k)) for t in live}
            for j in range(PANEL)
        ]
        rows = [tiles[home][first % 8 + j : first % 8 + j + 1, :] for j in range(PANEL)]
        for j in range(PANEL):
            at = first % 8 + j
            inverse = 1.0 / columns[j][home][at : at + 1, :]
            factors = {t: columns[j][t] * inverse for t in live}
            factors[home] = jnp.where(sub > at, factors[home], 0.0)
            for later in range(j + 1, PANEL):
                cross = columns[later][home][at : at + 1, :]
                for t in live:
                    columns[later][t] = columns[later][t] - factors[t] * cross
                where = first % 8 + later
                rows[later] = rows[later] - factors[home][where : where + 1, :] * rows[j]
            for t in live:
                tiles[t] = tiles[t] - factors[t] * rows[j]
    scaled = []
    for t in range(k // 8):
        diagonal = jnp.sum(jnp.where(lane == sub + 8 * t, tiles[t], 0.0), axis=1, keepdims=True)
        scaled.append(jnp.where(lane < k, 0.0, tiles[t]) * lax.rsqrt(diagonal))
    inverse_factor = jnp.concatenate(scaled, axis=0)
    return jnp.dot(
        inverse_factor,
        jnp.concatenate([zeros, cov], axis=0),
        precision=lax.Precision.HIGHEST,
        preferred_element_type=F32,
    )


def kernel(
    n, scale,
    expr_ref, dos_ref, cov_ref,
    out_ref,
    cov_v, dos_v, vt, graw, g_own, g_left, g_right, p_own, p_left, p_right, q6, qd, qt6,
    local_sem, a2a_send, a2a_recv, g_send, g_recv, p_send, p_recv,
):
    me = lax.axis_index("blk")
    samples, width = dos_v.shape
    part = expr_ref.shape[0]
    panels = width // BS
    k = cov_v.shape[0]

    cov_copy = pltpu.make_async_copy(cov_ref, cov_v, local_sem.at[0])
    cov_copy.start()
    dos_copy = pltpu.make_async_copy(dos_ref, dos_v, local_sem.at[1])
    dos_copy.start()

    def columns_of(j):
        return expr_ref.at[:, pl.ds(pl.multiple_of(j * BS, BS), BS)]

    mine = graw.at[pl.ds(pl.multiple_of(me * part, 16), part), :]
    own_copy = pltpu.make_async_copy(columns_of(me), mine, local_sem.at[2])
    own_copy.start()

    barrier = pltpu.get_barrier_semaphore()

    @pl.loop(1, n)
    def _(s):
        pl.semaphore_signal(
            barrier, inc=1, device_id={"blk": lax.rem(me + s, n)}, device_id_type=MESH
        )

    pl.semaphore_wait(barrier, n - 1)

    def exchange(s):
        peer = lax.rem(me + s, n)
        return pltpu.make_async_remote_copy(
            src_ref=columns_of(peer),
            dst_ref=mine,
            send_sem=a2a_send.at[s],
            recv_sem=a2a_recv.at[s],
            device_id={"blk": peer},
            device_id_type=MESH,
        )

    @pl.loop(1, n)
    def _(s):
        exchange(s).start()

    cov_copy.wait()
    dos_copy.wait()

    @pl.loop(0, panels)
    def _(c):
        at = pl.multiple_of(c * BS, BS)
        vt[pl.ds(at, BS), :] = dos_v[:, pl.ds(at, BS)].T

    q = whitened(cov_v[...])
    qh, qm, ql = split3(q)
    q6[...] = jnp.concatenate([qh, qm, qh, qm, qh, ql], axis=0)
    qd[...] = jnp.concatenate([qh, qh, qm, qm, ql, ql], axis=0)
    first = q6[0 : 2 * k, :].T
    qt6[:, 0 : 2 * k] = first
    qt6[:, 2 * k : 4 * k] = first
    qt6[:, 4 * k : 6 * k] = q6[4 * k : 6 * k, :].T

    @pl.loop(0, panels)
    def _(c):
        at = pl.multiple_of(c * BS, BS)
        v = vt[pl.ds(at, BS), :]
        w3 = lax.dot_general(v, qd[...], NT, preferred_element_type=F32)
        w = w3[:, 0 : 2 * k] + w3[:, 2 * k : 4 * k] + w3[:, 4 * k : 6 * k]
        wh, wm, wl = split3(w)
        lane = lax.broadcasted_iota(jnp.int32, w.shape, 1)
        last = jnp.where(lane < k, wl.astype(F32), wh.astype(F32)).astype(BF16)
        w6 = jnp.concatenate([wh, wm, last], axis=1)
        res = v.astype(F32) - jnp.dot(w6, q6[...], preferred_element_type=F32)
        mean = jnp.sum(res * res, axis=1, keepdims=True) * (1.0 / samples)
        vt[pl.ds(at, BS), :] = (res * lax.rsqrt(mean + 1e-06)).astype(BF16)

    own_copy.wait()

    @pl.loop(1, n)
    def _(s):
        exchange(s).wait_recv()

    g = graw[...]
    w3 = jnp.dot(
        jnp.concatenate([q6[0 : 2 * k, :], q6[5 * k : 6 * k, :]], axis=0),
        g,
        preferred_element_type=F32,
    )
    wh, wm, wl = split3(w3[0:k, :] + w3[k : 2 * k, :] + w3[2 * k : 3 * k, :])
    w6 = jnp.concatenate([wh, wh, wm, wm, wl, wh], axis=0)
    res = g.astype(F32) - jnp.dot(qt6[...], w6, preferred_element_type=F32)
    mean = jnp.sum(res * res, axis=0, keepdims=True) * (1.0 / samples)
    g_own[...] = (res * lax.rsqrt(mean + 1e-06)).astype(BF16)

    def send(src, dst, sems, slot, peer):
        return pltpu.make_async_remote_copy(
            src_ref=src,
            dst_ref=dst,
            send_sem=sems[0].at[slot],
            recv_sem=sems[1].at[slot],
            device_id={"blk": peer},
            device_id_type=MESH,
        )

    genes_left = send(g_own, g_right, (g_send, g_recv), 0, me - 1)
    genes_right = send(g_own, g_left, (g_send, g_recv), 1, me + 1)
    back_left = send(
        p_left, out_ref.at[pl.ds(2 * width, width), :], (p_send, p_recv), 0, me - 1
    )
    back_right = send(p_right, out_ref.at[pl.ds(0, width), :], (p_send, p_recv), 1, me + 1)
    has_left = me > 0
    has_right = me < n - 1

    @pl.when(has_left)
    def _():
        genes_left.start()

    @pl.when(has_right)
    def _():
        genes_right.start()

    def multiply(genes, target):
        @pl.loop(0, panels // 2)
        def _(c):
            at = pl.multiple_of(c * 2 * BS, 2 * BS)
            product = jnp.dot(
                vt[pl.ds(at, 2 * BS), :], genes[...], preferred_element_type=F32
            )
            target[pl.ds(at, 2 * BS), :] = (product * scale).astype(BF16)

    multiply(g_own, p_own)
    keep = pltpu.make_async_copy(p_own, out_ref.at[pl.ds(width, width), :], local_sem.at[3])
    keep.start()

    @pl.when(has_left)
    def _():
        genes_right.wait_recv()
        multiply(g_left, p_left)
        back_left.start()

    @pl.when(has_right)
    def _():
        genes_left.wait_recv()
        multiply(g_right, p_right)
        back_right.start()

    keep.wait()

    @pl.loop(1, n)
    def _(s):
        exchange(s).wait_send()

    @pl.when(has_left)
    def _():
        genes_left.wait_send()
        back_left.wait_send()
        back_right.wait_recv()

    @pl.when(has_right)
    def _():
        genes_right.wait_send()
        back_right.wait_send()
        back_left.wait_recv()


def on_device(expression, dosages, covariates, window_blocks, window_counts):
    n = lax.axis_size("blk")
    samples, width = dosages.shape
    panels = width // BS
    k = covariates.shape[0]
    slots = window_blocks.shape[1]
    scale = math.sqrt(samples - k) / samples
    any_space = pl.BlockSpec(memory_space=pl.ANY)
    blocks = 3 * panels + slots
    products = pl.pallas_call(
        functools.partial(kernel, n, scale),
        out_shape=jax.ShapeDtypeStruct((blocks * BS, BS), BF16),
        in_specs=[any_space] * 3,
        out_specs=any_space,
        scratch_shapes=[
            pltpu.VMEM((k, samples), F32),
            pltpu.VMEM((samples, width), BF16),
            pltpu.VMEM((width, samples), BF16),
            pltpu.VMEM((samples, BS), BF16),
            pltpu.VMEM((samples, BS), BF16),
            pltpu.VMEM((samples, BS), BF16),
            pltpu.VMEM((samples, BS), BF16),
            pltpu.VMEM((width, BS), BF16),
            pltpu.VMEM((width, BS), BF16),
            pltpu.VMEM((width, BS), BF16),
            pltpu.VMEM((6 * k, samples), BF16),
            pltpu.VMEM((6 * k, samples), BF16),
            pltpu.VMEM((samples, 6 * k), BF16),
            pltpu.SemaphoreType.DMA((4,)),
            pltpu.SemaphoreType.DMA((n,)),
            pltpu.SemaphoreType.DMA((n,)),
            pltpu.SemaphoreType.DMA((2,)),
            pltpu.SemaphoreType.DMA((2,)),
            pltpu.SemaphoreType.DMA((2,)),
            pltpu.SemaphoreType.DMA((2,)),
        ],
        compiler_params=pltpu.CompilerParams(
            collective_id=0, has_side_effects=True, vmem_limit_bytes=50 * 1024 * 1024
        ),
    )(expression, dosages, covariates)
    first = window_blocks[0, 0] - (lax.axis_index("blk") - 1) * panels
    listed = lax.dynamic_slice_in_dim(products.reshape(blocks, BS, BS), first, slots, axis=0)
    live = jnp.arange(slots)[None, :] < window_counts[:, None]
    return jnp.where(live[:, :, None, None], listed[None].astype(F32), 0.0)


def solution(mesh):
    in_specs = (
        P("blk", "slab"),
        P(None, ("slab", "blk")),
        P(),
        P(("slab", "blk"), None),
        P(("slab", "blk")),
    )
    out_specs = P(("slab", "blk"), None, None, None)
    return jax.shard_map(
        on_device, mesh=mesh, in_specs=in_specs, out_specs=out_specs, check_vma=False
    )
```

time: 76.7 us -> 35.5 us (0.46); the launches traced: 75.4 us -> 35.3 us
  Pallas kernels: 0 us -> 29.6 us
  waiting for transfers between devices: 26.4 us -> 0 us
  other arithmetic: 17.2 us -> 1.12 us
  starting transfers between devices: 12.9 us -> 0 us
  matrix products: 12 us -> 0 us
  local copies, waits for them, and re-layouts: 5.99 us -> 3.26 us
    pallas_call x0 -> x1, Pallas kernels: none -> 29.6 us  [on_device(): pl.pallas_call(functools.partial(kernel, n, scale), out_shape=jax.ShapeDt...]
    all_to_all x1 -> x0, waiting for transfers between devices: 26.4 us -> none  [on_device(): lax.all_to_all(expression, 'blk', split_axis=1, concat_axis=0, tiled=True)]
    another operation x5 -> x0, other arithmetic: 12.2 us -> none  [the longest x3 6.6 us: on_device(): jnp.linalg.cholesky(jnp.dot(covariates, covariates.T, precision=lax.Preci...]
    dot_general x6 -> x0, matrix products: 9.88 us -> none  [the longest x2 4.24 us: residualize(): jnp.dot(covariates.T, coefficients, precision=lax.Precision.HIGHEST)]
    ppermute x2 -> x0, starting transfers between devices: 6.46 us -> none  [the longest x1 4.54 us: extended_2(): lax.ppermute(lax.slice_in_dim(block, block.shape[dim] - width, None, axis...]
    all_to_all x1 -> x0, starting transfers between devices: 6.45 us -> none  [on_device(): lax.all_to_all(expression, 'blk', split_axis=1, concat_axis=0, tiled=True)]
    concatenate x1 -> x0, other arithmetic: 3.87 us -> none  [extended_2(): block = jnp.concatenate([low, block, high], axis=dim)]
    gather x1 -> x0, local copies, waits for them, and re-layouts: 3.08 us -> none  [listed_products(): chosen = jnp.take(panels, local_index.reshape(-1), axis=1)]
  transfers between devices with their start and end apart: 3 -> 0, of which waited for: 1 -> 0; matrix products, arithmetic and copies ran while one was open for 4% -> 0% of each run, Pallas kernels for 0% -> 0%
where the time goes in v1:
time: 35.5 us; the launch traced here: 35.3 us
  Pallas kernels  29.6 us (83%)
  local copies, waits for them, and re-layouts  3.26 us (9%)
  between operations  1.33 us (4%)
  other arithmetic  1.12 us (3%)
    pallas_call x1, Pallas kernels, on_device(): pl.pallas_call(functools.partial(kernel, n, scale), out_shape=jax.ShapeDt...  29.6 us
    unnamed x6, local copies, waits for them, and re-layouts  3.26 us
    select_n x1, other arithmetic, on_device(): return jnp.where(live[:, :, None, None], listed[None].astype(F32), 0.0)  1.12 us

profile of v1, /device:TPU:1, one launch (start us, length us, event | category | flops | bytes accessed | tf_op | source)
XLA Modules:
  0.0 35.3 jit_solution(9194662980649962392)
XLA Ops:
  1.3 0.0 copy-start
  1.3 1.4 %copy-done = bf16[768,1024]{1,0:T(8,128)(2,1)S(1)} copy-done((bf16[768,1024]{1,0:T(8,128)(2,1)S(1)}, bf16[768,1024]{1,0:T(8,128)(2,1)}, u32[]{:S(2)}) %copy-start) | copy-done | bytes 1572888
  2.7 0.0 copy-start.1
  2.7 0.9 %copy-done.1 = bf16[48,2048]{1,0:T(8,128)(2,1)S(1)} copy-done((bf16[48,2048]{1,0:T(8,128)(2,1)S(1)}, bf16[48,2048]{1,0:T(8,128)(2,1)}, u32[]{:S(2)}) %copy-start.1) | copy-done | bytes 196632
  3.7 0.0 copy-start.2
  3.7 0.9 %copy-done.2 = f32[64,768]{1,0:T(8,128)S(1)} copy-done((f32[64,768]{1,0:T(8,128)S(1)}, f32[64,768]{1,0:T(8,128)}, u32[]{:S(2)}) %copy-start.2) | copy-done | bytes 196632
  4.6 29.6 %shard_map.55 = bf16[5120,128]{1,0:T(8,128)(2,1)S(1)} custom-call(bf16[48,2048]{1,0:T(8,128)(2,1)S(1)} %copy-done.1, bf16[768,1024]{1,0:T(8,128)(2,1)S(1)} %copy-done, f32[64,768]{1,0:T(8,128)S(1)} %copy-done.2), custom_call_target="tpu_custom_call" | custom-call | tf_op jit(solution)/shard_map/pallas_call | solution.py:256
  34.2 1.1 %select_bitcast_fusion = f32[1,16,128,128]{3,2,1,0:T(8,128)} fusion(bf16[40,128,128]{2,1,0:T(8,128)(2,1)S(1)} %bitcast.7, s32[]{:T(128)S(6)} %select_n.10, pred[16]{0:T(512)(128)(4,1)S(1)} %iota_compare_fusion), kind=kLoop, calls=%fused_computation | loop fusion | flops 524288 | bytes 1572884 | tf_op jit(solution)/shard_map/jit(_where)/select_n | solution.py:290
  (1 shorter events, 0.0 us)
Async XLA Ops:
  1.3 1.4 %copy-start = (bf16[768,1024]{1,0:T(8,128)(2,1)S(1)}, bf16[768,1024]{1,0:T(8,128)(2,1)}, u32[]{:S(2)}) copy-start(bf16[768,1024]{1,0:T(8,128)(2,1)} %dos_ref.1) | copy-start | bytes 4718596
  2.7 0.9 %copy-start.1 = (bf16[48,2048]{1,0:T(8,128)(2,1)S(1)}, bf16[48,2048]{1,0:T(8,128)(2,1)}, u32[]{:S(2)}) copy-start(bf16[48,2048]{1,0:T(8,128)(2,1)} %expr_ref.1) | copy-start | bytes 589828
  3.7 0.9 %copy-start.2 = (f32[64,768]{1,0:T(8,128)S(1)}, f32[64,768]{1,0:T(8,128)}, u32[]{:S(2)}) copy-start(f32[64,768]{1,0:T(8,128)} %cov_ref.1) | copy-start | bytes 589828

commit v2 on v1

--- a/solution.py
+++ b/solution.py
@@ -10,6 +10,8 @@
 
 BS = 128
 PANEL = 4
+ROWS = 256
+VMEM_BYTES = 63 * 10**6
 MESH = pl.DeviceIdType.MESH
 F32 = jnp.float32
 BF16 = jnp.bfloat16
@@ -75,63 +77,59 @@
 
 
 def kernel(
-    n, scale,
+    n, scale, rows,
     expr_ref, dos_ref, cov_ref,
     out_ref,
-    cov_v, dos_v, vt, graw, g_own, g_left, g_right, p_own, p_left, p_right, q6, qd, qt6,
+    cov_v, dos_v, vt, graw, p_own, p_left, p_right, q6, qd, qt6,
     local_sem, a2a_send, a2a_recv, g_send, g_recv, p_send, p_recv,
 ):
     me = lax.axis_index("blk")
     samples, width = dos_v.shape
     part = expr_ref.shape[0]
-    panels = width // BS
     k = cov_v.shape[0]
+    has_left = me > 0
+    has_right = me < n - 1
+
+    def columns_of(j):
+        return expr_ref.at[:, pl.ds(pl.multiple_of(j * BS, BS), BS)]
+
+    barrier = pltpu.get_barrier_semaphore()
+
+    @pl.loop(1, n)
+    def _(s):
+        pl.semaphore_signal(
+            barrier, inc=1, device_id={"blk": lax.rem(me + s, n)}, device_id_type=MESH
+        )
 
     cov_copy = pltpu.make_async_copy(cov_ref, cov_v, local_sem.at[0])
     cov_copy.start()
     dos_copy = pltpu.make_async_copy(dos_ref, dos_v, local_sem.at[1])
     dos_copy.start()
-
-    def columns_of(j):
-        return expr_ref.at[:, pl.ds(pl.multiple_of(j * BS, BS), BS)]
-
-    mine = graw.at[pl.ds(pl.multiple_of(me * part, 16), part), :]
+    mine = graw.at[1, pl.ds(pl.multiple_of(me * part, 16), part), :]
     own_copy = pltpu.make_async_copy(columns_of(me), mine, local_sem.at[2])
     own_copy.start()
 
-    barrier = pltpu.get_barrier_semaphore()
-
-    @pl.loop(1, n)
-    def _(s):
-        pl.semaphore_signal(
-            barrier, inc=1, device_id={"blk": lax.rem(me + s, n)}, device_id_type=MESH
-        )
-
-    pl.semaphore_wait(barrier, n - 1)
+    def remote(src, dst, sems, slot, peer):
+        return pltpu.make_async_remote_copy(
+            src_ref=src,
+            dst_ref=dst,
+            send_sem=sems[0].at[slot],
+            recv_sem=sems[1].at[slot],
+            device_id={"blk": peer},
+            device_id_type=MESH,
+        )
 
     def exchange(s):
         peer = lax.rem(me + s, n)
-        return pltpu.make_async_remote_copy(
-            src_ref=columns_of(peer),
-            dst_ref=mine,
-            send_sem=a2a_send.at[s],
-            recv_sem=a2a_recv.at[s],
-            device_id={"blk": peer},
-            device_id_type=MESH,
-        )
+        return remote(columns_of(peer), mine, (a2a_send, a2a_recv), s, peer)
+
+    pl.semaphore_wait(barrier, n - 1)
 
     @pl.loop(1, n)
     def _(s):
         exchange(s).start()
 
     cov_copy.wait()
-    dos_copy.wait()
-
-    @pl.loop(0, panels)
-    def _(c):
-        at = pl.multiple_of(c * BS, BS)
-        vt[pl.ds(at, BS), :] = dos_v[:, pl.ds(at, BS)].T
-
     q = whitened(cov_v[...])
     qh, qm, ql = split3(q)
     q6[...] = jnp.concatenate([qh, qm, qh, qm, qh, ql], axis=0)
@@ -141,10 +139,10 @@
     qt6[:, 2 * k : 4 * k] = first
     qt6[:, 4 * k : 6 * k] = q6[4 * k : 6 * k, :].T
 
-    @pl.loop(0, panels)
-    def _(c):
-        at = pl.multiple_of(c * BS, BS)
-        v = vt[pl.ds(at, BS), :]
+    dos_copy.wait()
+
+    def variants(at):
+        v = dos_v[:, pl.ds(at, rows)].T
         w3 = lax.dot_general(v, qd[...], NT, preferred_element_type=F32)
         w = w3[:, 0 : 2 * k] + w3[:, 2 * k : 4 * k] + w3[:, 4 * k : 6 * k]
         wh, wm, wl = split3(w)
@@ -153,7 +151,13 @@
         w6 = jnp.concatenate([wh, wm, last], axis=1)
         res = v.astype(F32) - jnp.dot(w6, q6[...], preferred_element_type=F32)
         mean = jnp.sum(res * res, axis=1, keepdims=True) * (1.0 / samples)
-        vt[pl.ds(at, BS), :] = (res * lax.rsqrt(mean + 1e-06)).astype(BF16)
+        vt[pl.ds(at, rows), :] = (res * lax.rsqrt(mean + 1e-06)).astype(BF16)
+
+    half = width // 2
+
+    @pl.loop(0, half // rows)
+    def _(c):
+        variants(pl.multiple_of(c * rows, rows))
 
     own_copy.wait()
 
@@ -161,36 +165,8 @@
     def _(s):
         exchange(s).wait_recv()
 
-    g = graw[...]
-    w3 = jnp.dot(
-        jnp.concatenate([q6[0 : 2 * k, :], q6[5 * k : 6 * k, :]], axis=0),
-        g,
-        preferred_element_type=F32,
-    )
-    wh, wm, wl = split3(w3[0:k, :] + w3[k : 2 * k, :] + w3[2 * k : 3 * k, :])
-    w6 = jnp.concatenate([wh, wh, wm, wm, wl, wh], axis=0)
-    res = g.astype(F32) - jnp.dot(qt6[...], w6, preferred_element_type=F32)
-    mean = jnp.sum(res * res, axis=0, keepdims=True) * (1.0 / samples)
-    g_own[...] = (res * lax.rsqrt(mean + 1e-06)).astype(BF16)
-
-    def send(src, dst, sems, slot, peer):
-        return pltpu.make_async_remote_copy(
-            src_ref=src,
-            dst_ref=dst,
-            send_sem=sems[0].at[slot],
-            recv_sem=sems[1].at[slot],
-            device_id={"blk": peer},
-            device_id_type=MESH,
-        )
-
-    genes_left = send(g_own, g_right, (g_send, g_recv), 0, me - 1)
-    genes_right = send(g_own, g_left, (g_send, g_recv), 1, me + 1)
-    back_left = send(
-        p_left, out_ref.at[pl.ds(2 * width, width), :], (p_send, p_recv), 0, me - 1
-    )
-    back_right = send(p_right, out_ref.at[pl.ds(0, width), :], (p_send, p_recv), 1, me + 1)
-    has_left = me > 0
-    has_right = me < n - 1
+    genes_left = remote(graw.at[1], graw.at[2], (g_send, g_recv), 0, me - 1)
+    genes_right = remote(graw.at[1], graw.at[0], (g_send, g_recv), 1, me + 1)
 
     @pl.when(has_left)
     def _():
@@ -200,30 +176,76 @@
     def _():
         genes_right.start()
 
-    def multiply(genes, target):
-        @pl.loop(0, panels // 2)
-        def _(c):
-            at = pl.multiple_of(c * 2 * BS, 2 * BS)
-            product = jnp.dot(
-                vt[pl.ds(at, 2 * BS), :], genes[...], preferred_element_type=F32
-            )
-            target[pl.ds(at, 2 * BS), :] = (product * scale).astype(BF16)
-
-    multiply(g_own, p_own)
+    @pl.loop(half // rows, width // rows)
+    def _(c):
+        variants(pl.multiple_of(c * rows, rows))
+
+    def genes(raw):
+        w3 = jnp.dot(
+            jnp.concatenate([q6[0 : 2 * k, :], q6[5 * k : 6 * k, :]], axis=0),
+            raw,
+            preferred_element_type=F32,
+        )
+        wh, wm, wl = split3(w3[0:k, :] + w3[k : 2 * k, :] + w3[2 * k : 3 * k, :])
+        w6 = jnp.concatenate([wh, wh, wm, wm, wl, wh], axis=0)
+        res = raw.astype(F32) - jnp.dot(qt6[...], w6, preferred_element_type=F32)
+        mean = jnp.sum(res * res, axis=0, keepdims=True) * (1.0 / samples)
+        return (res * lax.rsqrt(mean + 1e-06)).astype(BF16)
+
+    pieces = 4
+    step = width // pieces
+
+    own = genes(graw[1])
+    for c in range(pieces):
+        product = jnp.dot(vt[c * step : (c + 1) * step, :], own, preferred_element_type=F32)
+        p_own[c * step : (c + 1) * step, :] = (product * scale).astype(BF16)
     keep = pltpu.make_async_copy(p_own, out_ref.at[pl.ds(width, width), :], local_sem.at[3])
     keep.start()
 
     @pl.when(has_left)
     def _():
         genes_right.wait_recv()
-        multiply(g_left, p_left)
-        back_left.start()
 
     @pl.when(has_right)
     def _():
         genes_left.wait_recv()
-        multiply(g_right, p_right)
-        back_right.start()
+
+    @pl.when(jnp.logical_not(has_left))
+    def _():
+        graw[0] = graw[1]
+
+    @pl.when(jnp.logical_not(has_right))
+    def _():
+        graw[2] = graw[1]
+
+    def back_left(c):
+        return remote(
+            p_left.at[pl.ds(c * step, step), :],
+            out_ref.at[pl.ds(2 * width + c * step, step), :],
+            (p_send, p_recv), c, me - 1,
+        )
+
+    def back_right(c):
+        return remote(
+            p_right.at[pl.ds(c * step, step), :],
+            out_ref.at[pl.ds(c * step, step), :],
+            (p_send, p_recv), pieces + c, me + 1,
+        )
+
+    both = genes(jnp.concatenate([graw[0], graw[2]], axis=1))
+    for c in range(pieces):
+        product = jnp.dot(vt[c * step : (c + 1) * step, :], both, preferred_element_type=F32)
+        product = (product * scale).astype(BF16)
+        p_left[c * step : (c + 1) * step, :] = product[:, 0:BS]
+        p_right[c * step : (c + 1) * step, :] = product[:, BS : 2 * BS]
+
+        @pl.when(has_left)
+        def _():
+            back_left(c).start()
+
+        @pl.when(has_right)
+        def _():
+            back_right(c).start()
 
     keep.wait()
 
@@ -234,14 +256,16 @@
     @pl.when(has_left)
     def _():
         genes_left.wait_send()
-        back_left.wait_send()
-        back_right.wait_recv()
+        for c in range(pieces):
+            back_left(c).wait_send()
+            back_right(c).wait_recv()
 
     @pl.when(has_right)
     def _():
         genes_right.wait_send()
-        back_right.wait_send()
-        back_left.wait_recv()
+        for c in range(pieces):
+            back_right(c).wait_send()
+            back_left(c).wait_recv()
 
 
 def on_device(expression, dosages, covariates, window_blocks, window_counts):
@@ -254,7 +278,7 @@
     any_space = pl.BlockSpec(memory_space=pl.ANY)
     blocks = 3 * panels + slots
     products = pl.pallas_call(
-        functools.partial(kernel, n, scale),
+        functools.partial(kernel, n, scale, ROWS),
         out_shape=jax.ShapeDtypeStruct((blocks * BS, BS), BF16),
         in_specs=[any_space] * 3,
         out_specs=any_space,
@@ -262,10 +286,7 @@
             pltpu.VMEM((k, samples), F32),
             pltpu.VMEM((samples, width), BF16),
             pltpu.VMEM((width, samples), BF16),
-            pltpu.VMEM((samples, BS), BF16),
-            pltpu.VMEM((samples, BS), BF16),
-            pltpu.VMEM((samples, BS), BF16),
-            pltpu.VMEM((samples, BS), BF16),
+            pltpu.VMEM((3, samples, BS), BF16),
             pltpu.VMEM((width, BS), BF16),
             pltpu.VMEM((width, BS), BF16),
             pltpu.VMEM((width, BS), BF16),
@@ -277,11 +298,11 @@
             pltpu.SemaphoreType.DMA((n,)),
             pltpu.SemaphoreType.DMA((2,)),
             pltpu.SemaphoreType.DMA((2,)),
-            pltpu.SemaphoreType.DMA((2,)),
-            pltpu.SemaphoreType.DMA((2,)),
+            pltpu.SemaphoreType.DMA((8,)),
+            pltpu.SemaphoreType.DMA((8,)),
         ],
         compiler_params=pltpu.CompilerParams(
-            collective_id=0, has_side_effects=True, vmem_limit_bytes=50 * 1024 * 1024
+            collective_id=0, has_side_effects=True, vmem_limit_bytes=VMEM_BYTES
         ),
     )(expression, dosages, covariates)
     first = window_blocks[0, 0] - (lax.axis_index("blk") - 1) * panels

time: 35.5 us -> 28.3 us (0.80)
  Pallas kernels: 29.6 us -> 24.3 us
  local copies, waits for them, and re-layouts: 3.26 us -> 0 us
  other arithmetic: 1.12 us -> 2.16 us
    pallas_call x1, Pallas kernels: 29.6 us -> 24.3 us  [on_device(): pl.pallas_call(functools.partial(kernel, n, scale, ROWS), out_shape=jax.S...]
    unnamed x6 -> x0, local copies, waits for them, and re-layouts: 3.26 us -> none
    select_n x1, other arithmetic: 1.12 us -> 2.16 us  [on_device(): return jnp.where(live[:, :, None, None], listed[None].astype(F32), 0.0)]
where the time goes in v2:
time: 28.3 us; the launch traced here: 27.8 us
  Pallas kernels  24.3 us (86%)
  other arithmetic  2.16 us (8%)
  between operations  1.32 us (5%)
    pallas_call x1, Pallas kernels, on_device(): pl.pallas_call(functools.partial(kernel, n, scale, ROWS), out_shape=jax.S...  24.3 us
    select_n x1, other arithmetic, on_device(): return jnp.where(live[:, :, None, None], listed[None].astype(F32), 0.0)  2.16 us

profile of v2, /device:TPU:1, one launch (start us, length us, event | category | flops | bytes accessed | tf_op | source)
XLA Modules:
  0.0 27.8 jit_solution(7589920444780666130)
XLA Ops:
  1.3 24.3 %shard_map.55 = bf16[5120,128]{1,0:T(8,128)(2,1)} custom-call(bf16[48,2048]{1,0:T(8,128)(2,1)} %expr_ref.1, bf16[768,1024]{1,0:T(8,128)(2,1)} %dos_ref.1, f32[64,768]{1,0:T(8,128)} %cov_ref.1), custom_call_target="tpu_custom_call" | custom-call | tf_op jit(solution)/shard_map/pallas_call | solution.py:280
  25.7 2.2 %select_bitcast_fusion = f32[1,16,128,128]{3,2,1,0:T(8,128)} fusion(bf16[40,128,128]{2,1,0:T(8,128)(2,1)} %bitcast.7, s32[]{:T(128)S(6)} %select_n.10, pred[16]{0:T(512)(128)(4,1)S(1)} %iota_compare_fusion), kind=kLoop, calls=%fused_computation | loop fusion | flops 524288 | bytes 1572884 | tf_op jit(solution)/shard_map/jit(_where)/select_n | solution.py:311
  (1 shorter events, 0.0 us)

commit v3 on v2

--- a/solution.py
+++ b/solution.py
@@ -80,18 +80,22 @@
     n, scale, rows,
     expr_ref, dos_ref, cov_ref,
     out_ref,
-    cov_v, dos_v, vt, graw, p_own, p_left, p_right, q6, qd, qt6,
-    local_sem, a2a_send, a2a_recv, g_send, g_recv, p_send, p_recv,
+    cov_v, dos_v, vt, pair, ready, chip_ready, p_own, p_cross, p_chip, q6, qd, qt6,
+    local_sem, a2a_send, a2a_recv, edge_send, edge_recv, g_send, g_recv, p_send, p_recv,
 ):
     me = lax.axis_index("blk")
     samples, width = dos_v.shape
     part = expr_ref.shape[0]
     k = cov_v.shape[0]
-    has_left = me > 0
-    has_right = me < n - 1
-
-    def columns_of(j):
-        return expr_ref.at[:, pl.ds(pl.multiple_of(j * BS, BS), BS)]
+    odd = lax.rem(me, 2)
+    side = lax.rem(me // 2, 2)
+    cross = me - 1 + 2 * odd
+    chip = me + 1 - 2 * odd
+    at_edge = jnp.logical_or(me == 0, me == n - 1)
+    inside = jnp.logical_not(at_edge)
+    own_half = 1 - odd
+    fellows = n // 2
+    rank = (me // 4) * 2 + odd
 
     barrier = pltpu.get_barrier_semaphore()
 
@@ -105,9 +109,29 @@
     cov_copy.start()
     dos_copy = pltpu.make_async_copy(dos_ref, dos_v, local_sem.at[1])
     dos_copy.start()
-    mine = graw.at[1, pl.ds(pl.multiple_of(me * part, 16), part), :]
-    own_copy = pltpu.make_async_copy(columns_of(me), mine, local_sem.at[2])
-    own_copy.start()
+    my_rows = pl.ds(pl.multiple_of(me * part, 16), part)
+
+    def columns(j, count):
+        return expr_ref.at[:, pl.ds(pl.multiple_of(j * BS, BS), count * BS)]
+
+    def half(j):
+        return pl.ds(pl.multiple_of(j * BS, BS), BS)
+
+    own_pair = pltpu.make_async_copy(
+        columns(me - own_half, 2), pair.at[my_rows, :], local_sem.at[2]
+    )
+    own_single = pltpu.make_async_copy(
+        columns(me, 1), pair.at[my_rows, half(own_half)], local_sem.at[2]
+    )
+
+    @pl.when(inside)
+    def _():
+        own_pair.start()
+
+    @pl.when(at_edge)
+    def _():
+        own_single.start()
+        ready[odd] = jnp.zeros((samples, BS), BF16)
 
     def remote(src, dst, sems, slot, peer):
         return pltpu.make_async_remote_copy(
@@ -119,21 +143,50 @@
             device_id_type=MESH,
         )
 
-    def exchange(s):
-        peer = lax.rem(me + s, n)
-        return remote(columns_of(peer), mine, (a2a_send, a2a_recv), s, peer)
+    def peer_of(s):
+        index = lax.rem(rank + s, fellows)
+        return (index // 2) * 4 + 2 * side + lax.rem(index, 2)
+
+    def shard_pair(s):
+        peer = peer_of(s)
+        low = jnp.clip(peer - 1 + lax.rem(peer, 2), 0, n - 2)
+        return remote(columns(low, 2), pair.at[my_rows, :], (a2a_send, a2a_recv), s, peer)
+
+    def shard_single(s):
+        peer = peer_of(s)
+        target = pair.at[my_rows, half(1 - lax.rem(peer, 2))]
+        return remote(columns(peer, 1), target, (a2a_send, a2a_recv), s, peer)
+
+    def peer_at_edge(s):
+        peer = peer_of(s)
+        return jnp.logical_or(peer == 0, peer == n - 1)
+
+    far_edge = (1 - side) * (n - 1)
+    to_edge = remote(
+        columns(far_edge, 1),
+        pair.at[my_rows, half(side)],
+        (edge_send, edge_recv), rank, far_edge,
+    )
 
     pl.semaphore_wait(barrier, n - 1)
 
-    @pl.loop(1, n)
+    @pl.loop(1, fellows, unroll=True)
     def _(s):
-        exchange(s).start()
+        @pl.when(peer_at_edge(s))
+        def _():
+            shard_single(s).start()
+
+        @pl.when(jnp.logical_not(peer_at_edge(s)))
+        def _():
+            shard_pair(s).start()
+
+    to_edge.start()
 
     cov_copy.wait()
     q = whitened(cov_v[...])
     qh, qm, ql = split3(q)
     q6[...] = jnp.concatenate([qh, qm, qh, qm, qh, ql], axis=0)
-    qd[...] = jnp.concatenate([qh, qh, qm, qm, ql, ql], axis=0)
+    qd[...] = jnp.concatenate([qh, qm, ql, ql], axis=0)
     first = q6[0 : 2 * k, :].T
     qt6[:, 0 : 2 * k] = first
     qt6[:, 2 * k : 4 * k] = first
@@ -144,7 +197,8 @@
     def variants(at):
         v = dos_v[:, pl.ds(at, rows)].T
         w3 = lax.dot_general(v, qd[...], NT, preferred_element_type=F32)
-        w = w3[:, 0 : 2 * k] + w3[:, 2 * k : 4 * k] + w3[:, 4 * k : 6 * k]
+        w = w3[:, 0 : 2 * k]
+        w = w + pltpu.roll(w, k, 1) + w3[:, 2 * k : 4 * k]
         wh, wm, wl = split3(w)
         lane = lax.broadcasted_iota(jnp.int32, w.shape, 1)
         last = jnp.where(lane < k, wl.astype(F32), wh.astype(F32)).astype(BF16)
@@ -153,32 +207,50 @@
         mean = jnp.sum(res * res, axis=1, keepdims=True) * (1.0 / samples)
         vt[pl.ds(at, rows), :] = (res * lax.rsqrt(mean + 1e-06)).astype(BF16)
 
-    half = width // 2
-
-    @pl.loop(0, half // rows)
-    def _(c):
-        variants(pl.multiple_of(c * rows, rows))
-
-    own_copy.wait()
-
-    @pl.loop(1, n)
-    def _(s):
-        exchange(s).wait_recv()
-
-    genes_left = remote(graw.at[1], graw.at[2], (g_send, g_recv), 0, me - 1)
-    genes_right = remote(graw.at[1], graw.at[0], (g_send, g_recv), 1, me + 1)
-
-    @pl.when(has_left)
-    def _():
-        genes_left.start()
-
-    @pl.when(has_right)
-    def _():
-        genes_right.start()
-
-    @pl.loop(half // rows, width // rows)
-    def _(c):
-        variants(pl.multiple_of(c * rows, rows))
+    chips = n // 4
+
+    def stretch(i, which):
+        chunk = lax.rem(me // 4 + i, chips)
+        rows_at = pl.ds(pl.multiple_of((chunk * 4 + 2 * which) * part, 16), 2 * part)
+        return remote(
+            pair.at[rows_at, :], pair.at[rows_at, :], (g_send, g_recv), chunk, cross
+        )
+
+    def pass_on(i):
+        chunk = lax.rem(me // 4 + i, chips)
+        for member in range(2):
+            s = lax.rem(rank - chunk * 2 - member + fellows, fellows)
+
+            @pl.when(jnp.logical_and(s > 0, at_edge))
+            def _():
+                shard_single(s).wait_recv()
+
+            @pl.when(jnp.logical_and(s > 0, inside))
+            def _():
+                shard_pair(s).wait_recv()
+
+        @pl.when(inside)
+        def _():
+            stretch(i, side).start()
+
+    @pl.when(inside)
+    def _():
+        own_pair.wait()
+
+    @pl.when(at_edge)
+    def _():
+        own_single.wait()
+
+    quarter = width // 4
+    for c in range(4):
+
+        @pl.loop(2 * c * chips // 4 if c < 2 else chips, min(2 * c + 2, 4) * chips // 4)
+        def _(i):
+            pass_on(i)
+
+        @pl.loop(c * quarter // rows, (c + 1) * quarter // rows)
+        def _(t):
+            variants(pl.multiple_of(t * rows, rows))
 
     def genes(raw):
         w3 = jnp.dot(
@@ -192,80 +264,92 @@
         mean = jnp.sum(res * res, axis=0, keepdims=True) * (1.0 / samples)
         return (res * lax.rsqrt(mean + 1e-06)).astype(BF16)
 
+    @pl.when(inside)
+    def _():
+        @pl.loop(0, chips)
+        def _(i):
+            stretch(i, 1 - side).wait_recv()
+
+        both = genes(pair[...])
+        ready[0] = both[:, 0:BS]
+        ready[1] = both[:, BS : 2 * BS]
+
+    @pl.when(at_edge)
+    def _():
+        @pl.loop(0, fellows)
+        def _(i):
+            remote(
+                columns(far_edge, 1),
+                pair.at[my_rows, half(side)],
+                (edge_send, edge_recv), i, far_edge,
+            ).wait_recv()
+
+        ready[own_half] = genes(pair[:, half(own_half)])
+
+    share = remote(ready.at[own_half], chip_ready, (g_send, g_recv), chips, chip)
+    share.start()
+
     pieces = 4
     step = width // pieces
 
-    own = genes(graw[1])
+    def back_cross(c):
+        rows_at = pl.multiple_of(own_half * 2 * width + c * step, BS)
+        return remote(
+            p_cross.at[pl.ds(c * step, step), :],
+            out_ref.at[pl.ds(rows_at, step), :],
+            (p_send, p_recv), c, cross,
+        )
+
+    back_chip = remote(
+        p_chip,
+        out_ref.at[pl.ds(pl.multiple_of(odd * 2 * width, BS), width), :],
+        (p_send, p_recv), pieces, chip,
+    )
+
     for c in range(pieces):
-        product = jnp.dot(vt[c * step : (c + 1) * step, :], own, preferred_element_type=F32)
-        p_own[c * step : (c + 1) * step, :] = (product * scale).astype(BF16)
+        product = jnp.dot(
+            vt[c * step : (c + 1) * step, :], ready[odd], preferred_element_type=F32
+        )
+        p_cross[c * step : (c + 1) * step, :] = (product * scale).astype(BF16)
+
+        @pl.when(inside)
+        def _():
+            back_cross(c).start()
+
+    share.wait_recv()
+    local = jnp.concatenate([ready[own_half], chip_ready[...]], axis=1)
+    for c in range(pieces):
+        product = jnp.dot(vt[c * step : (c + 1) * step, :], local, preferred_element_type=F32)
+        product = (product * scale).astype(BF16)
+        p_own[c * step : (c + 1) * step, :] = product[:, 0:BS]
+        p_chip[c * step : (c + 1) * step, :] = product[:, BS : 2 * BS]
+    back_chip.start()
     keep = pltpu.make_async_copy(p_own, out_ref.at[pl.ds(width, width), :], local_sem.at[3])
     keep.start()
-
-    @pl.when(has_left)
-    def _():
-        genes_right.wait_recv()
-
-    @pl.when(has_right)
-    def _():
-        genes_left.wait_recv()
-
-    @pl.when(jnp.logical_not(has_left))
-    def _():
-        graw[0] = graw[1]
-
-    @pl.when(jnp.logical_not(has_right))
-    def _():
-        graw[2] = graw[1]
-
-    def back_left(c):
-        return remote(
-            p_left.at[pl.ds(c * step, step), :],
-            out_ref.at[pl.ds(2 * width + c * step, step), :],
-            (p_send, p_recv), c, me - 1,
-        )
-
-    def back_right(c):
-        return remote(
-            p_right.at[pl.ds(c * step, step), :],
-            out_ref.at[pl.ds(c * step, step), :],
-            (p_send, p_recv), pieces + c, me + 1,
-        )
-
-    both = genes(jnp.concatenate([graw[0], graw[2]], axis=1))
-    for c in range(pieces):
-        product = jnp.dot(vt[c * step : (c + 1) * step, :], both, preferred_element_type=F32)
-        product = (product * scale).astype(BF16)
-        p_left[c * step : (c + 1) * step, :] = product[:, 0:BS]
-        p_right[c * step : (c + 1) * step, :] = product[:, BS : 2 * BS]
-
-        @pl.when(has_left)
-        def _():
-            back_left(c).start()
-
-        @pl.when(has_right)
-        def _():
-            back_right(c).start()
-
     keep.wait()
 
-    @pl.loop(1, n)
+    @pl.loop(1, fellows, unroll=True)
     def _(s):
-        exchange(s).wait_send()
-
-    @pl.when(has_left)
-    def _():
-        genes_left.wait_send()
+        @pl.when(peer_at_edge(s))
+        def _():
+            shard_single(s).wait_send()
+
+        @pl.when(jnp.logical_not(peer_at_edge(s)))
+        def _():
+            shard_pair(s).wait_send()
+
+    to_edge.wait_send()
+    share.wait_send()
+    back_chip.wait()
+
+    @pl.when(inside)
+    def _():
+        @pl.loop(0, chips)
+        def _(i):
+            stretch(i, side).wait_send()
+
         for c in range(pieces):
-            back_left(c).wait_send()
-            back_right(c).wait_recv()
-
-    @pl.when(has_right)
-    def _():
-        genes_right.wait_send()
-        for c in range(pieces):
-            back_right(c).wait_send()
-            back_left(c).wait_recv()
+            back_cross(c).wait()
 
 
 def on_device(expression, dosages, covariates, window_blocks, window_counts):
@@ -286,20 +370,24 @@
             pltpu.VMEM((k, samples), F32),
             pltpu.VMEM((samples, width), BF16),
             pltpu.VMEM((width, samples), BF16),
-            pltpu.VMEM((3, samples, BS), BF16),
+            pltpu.VMEM((samples, 2 * BS), BF16),
+            pltpu.VMEM((2, samples, BS), BF16),
+            pltpu.VMEM((samples, BS), BF16),
             pltpu.VMEM((width, BS), BF16),
             pltpu.VMEM((width, BS), BF16),
             pltpu.VMEM((width, BS), BF16),
             pltpu.VMEM((6 * k, samples), BF16),
-            pltpu.VMEM((6 * k, samples), BF16),
+            pltpu.VMEM((4 * k, samples), BF16),
             pltpu.VMEM((samples, 6 * k), BF16),
             pltpu.SemaphoreType.DMA((4,)),
-            pltpu.SemaphoreType.DMA((n,)),
-            pltpu.SemaphoreType.DMA((n,)),
-            pltpu.SemaphoreType.DMA((2,)),
-            pltpu.SemaphoreType.DMA((2,)),
-            pltpu.SemaphoreType.DMA((8,)),
-            pltpu.SemaphoreType.DMA((8,)),
+            pltpu.SemaphoreType.DMA((n // 2,)),
+            pltpu.SemaphoreType.DMA((n // 2,)),
+            pltpu.SemaphoreType.DMA((n // 2,)),
+            pltpu.SemaphoreType.DMA((n // 2,)),
+            pltpu.SemaphoreType.DMA((n // 4 + 1,)),
+            pltpu.SemaphoreType.DMA((n // 4 + 1,)),
+            pltpu.SemaphoreType.DMA((5,)),
+            pltpu.SemaphoreType.DMA((5,)),
         ],
         compiler_params=pltpu.CompilerParams(
             collective_id=0, has_side_effects=True, vmem_limit_bytes=VMEM_BYTES

time: 28.3 us -> 27.1 us (0.958)
  the two profiles are of different devices: /device:TPU:1 before, /device:TPU:11 now
where the time goes in v3:
time: 27.1 us; the launch traced here: 26.9 us
  Pallas kernels  23.4 us (86%)
  other arithmetic  2.16 us (8%)
  between operations  1.32 us (5%)
    pallas_call x1, Pallas kernels, on_device(): pl.pallas_call(functools.partial(kernel, n, scale, ROWS), out_shape=jax.S...  23.4 us
    select_n x1, other arithmetic, on_device(): return jnp.where(live[:, :, None, None], listed[None].astype(F32), 0.0)  2.16 us

profile of v3, /device:TPU:11, one launch (start us, length us, event | category | flops | bytes accessed | tf_op | source)
XLA Modules:
  0.0 26.9 jit_solution(7826620735199870052)
XLA Ops:
  1.3 23.4 %shard_map.55 = bf16[5120,128]{1,0:T(8,128)(2,1)} custom-call(bf16[48,2048]{1,0:T(8,128)(2,1)} %expr_ref.1, bf16[768,1024]{1,0:T(8,128)(2,1)} %dos_ref.1, f32[64,768]{1,0:T(8,128)} %cov_ref.1), custom_call_target="tpu_custom_call" | custom-call | tf_op jit(solution)/shard_map/pallas_call | solution.py:364
  24.7 2.2 %select_bitcast_fusion = f32[1,16,128,128]{3,2,1,0:T(8,128)} fusion(bf16[40,128,128]{2,1,0:T(8,128)(2,1)} %bitcast.7, s32[]{:T(128)S(6)} %select_n.10, pred[16]{0:T(512)(128)(4,1)S(1)} %iota_compare_fusion), kind=kLoop, calls=%fused_computation | loop fusion | flops 524288 | bytes 1572884 | tf_op jit(solution)/shard_map/jit(_where)/select_n | solution.py:399
  (1 shorter events, 0.0 us)
